TPU v7x, 256 devices: a whole 4x4x8 slice. The times are simulated.
256 devices in a mesh: dp: 16 (over z, core), expert: 16 (over y, x).
Axes of the slice: x: 4, y: 4, z: 8, core: 2. Of those that a mesh axis runs over, the one named last changes fastest.
Arguments:
- tokens: bfloat16 [32768, 2048], P(('dp', 'expert')), may hold values from -6 to 6
- grad_out: bfloat16 [32768, 2048], P(('dp', 'expert')), may hold values from -6 to 6
- routes: int32 [32768, 4], P(('dp', 'expert')), may hold values from 0 to 15, all different within a row; in each aligned block of 128 rows (0 to 127, 128 to 255, ...) at most 40 rows name the same one
- combine: float32 [32768, 4], P(('dp', 'expert')), may hold values from 0.1 to 1
- w_gate: bfloat16 [16, 2048, 704], P('expert'), may hold values from -0.125 to 0.125
- w_up: bfloat16 [16, 2048, 704], P('expert'), may hold values from -0.125 to 0.125
- w_down: bfloat16 [16, 2048, 704], P('expert'), may hold values from -0.21875 to 0.21875
Outputs:
- grad_tokens: bfloat16 [32768, 2048], P(('dp', 'expert'))
- grad_gate: float32 [16, 2048, 704], P('expert', 'dp')
- grad_upper: float32 [16, 2048, 704], P('expert', 'dp')
- grad_down: float32 [16, 2048, 704], P('expert', 'dp')
Inputs may be any that keep to these rules, and one draw needn't show every extreme that they name: `routes`: within the rows of one device (aligned blocks of 128 tokens), no expert is named more than 40 times, a bound that some block reaches; a token's 4 experts differ.
All inputs are finite; a program needn't handle non-finite values.
Results may differ from a plain program's by a relative error of at most 0.023.
Values may be sent and summed in bfloat16 or wider, within the bound.
A program may use at most 320 MiB of HBM per device.

v0:
```python
import jax
import jax.numpy as jnp
from jax import lax
from jax.sharding import PartitionSpec as P


def expert_terms(rows_in, rows_cot, wg, wu, wd):
    gate = jnp.dot(rows_in, wg, preferred_element_type=jnp.float32)
    upper = jnp.dot(rows_in, wu, preferred_element_type=jnp.float32)
    sigma = jax.nn.sigmoid(gate)
    active = gate * sigma
    hidden = (active * upper).astype(jnp.bfloat16)
    grad_hidden = jnp.dot(rows_cot, wd, preferred_element_type=jnp.float32)
    grad_g = (grad_hidden * upper * sigma * (1.0 + gate * (1.0 - sigma))).astype(jnp.bfloat16)
    grad_u = (grad_hidden * active).astype(jnp.bfloat16)
    back = lax.dot_general(grad_g, wg, (((1,), (1,)), ((), ())), preferred_element_type=jnp.float32)
    back = back + lax.dot_general(
        grad_u, wu, (((1,), (1,)), ((), ())), preferred_element_type=jnp.float32
    )
    return (hidden, grad_g, grad_u, back.astype(jnp.bfloat16))


def weight_terms(inputs_cols, cot_cols, grad_g, grad_u, hidden):
    dims = (((0,), (0,)), ((), ()))
    first = lax.dot_general(inputs_cols, grad_g, dims, preferred_element_type=jnp.float32)
    second = lax.dot_general(inputs_cols, grad_u, dims, preferred_element_type=jnp.float32)
    third = lax.dot_general(cot_cols, hidden, dims, preferred_element_type=jnp.float32)
    return jnp.concatenate([first, second, third], axis=1)


def local(tokens, grad_out, routes, combine, w_gate, w_up, w_down):
    groups = lax.axis_size("expert")
    tok_rows = tokens.shape[0]
    width = tokens.shape[1]
    choose = routes.shape[1]
    hid_units = w_gate.shape[2]
    capacity = min(tok_rows, tok_rows * choose * 5 // (4 * groups))
    flat_e = routes.reshape(-1)
    onehot = (flat_e[:, None] == jnp.arange(groups, dtype=jnp.int32)[None, :]).astype(jnp.int32)
    before = jnp.cumsum(onehot, axis=0) - onehot
    slot = jnp.sum(before * onehot, axis=1)
    position = flat_e * capacity + slot
    repeated = jnp.repeat(tokens, choose, axis=0)
    scaled = (
        combine.reshape(-1)[:, None] * jnp.repeat(grad_out, choose, axis=0).astype(jnp.float32)
    ).astype(jnp.bfloat16)
    send_in = jnp.zeros((groups * capacity, width), jnp.bfloat16).at[position].set(repeated)
    send_cot = jnp.zeros((groups * capacity, width), jnp.bfloat16).at[position].set(scaled)
    recv_in, recv_cot = (
        lax.all_to_all(
            send_in.reshape(groups, capacity, width),
            "expert",
            split_axis=0,
            concat_axis=0,
            tiled=True,
        ),
        lax.all_to_all(
            send_cot.reshape(groups, capacity, width),
            "expert",
            split_axis=0,
            concat_axis=0,
            tiled=True,
        ),
    )
    rows_in = recv_in.reshape(groups * capacity, width)
    rows_cot = recv_cot.reshape(groups * capacity, width)
    hidden, grad_g, grad_u, back = expert_terms(rows_in, rows_cot, w_gate[0], w_up[0], w_down[0])
    returned = lax.all_to_all(
        back.reshape(groups, capacity, width), "expert", split_axis=0, concat_axis=0, tiled=True
    )
    picked = returned.reshape(groups * capacity, width)[position].astype(jnp.float32)
    grad_tokens = jnp.sum(picked.reshape(tok_rows, choose, width), axis=1).astype(jnp.bfloat16)
    terms = weight_terms(rows_in, rows_cot, grad_g, grad_u, hidden)
    summed = lax.psum_scatter(
        terms.astype(jnp.bfloat16), "dp", scatter_dimension=0, tiled=True
    ).astype(jnp.float32)
    grad_gate = summed[None, :, 0:hid_units]
    grad_upper = summed[None, :, hid_units : 2 * hid_units]
    grad_down = summed[None, :, 2 * hid_units : 3 * hid_units]
    return (grad_tokens, grad_gate, grad_upper, grad_down)


def solution(mesh):
    placed = (
        P(("dp", "expert"), None),
        P(("dp", "expert"), None),
        P(("dp", "expert"), None),
        P(("dp", "expert"), None),
        P("expert", None, None),
        P("expert", None, None),
        P("expert", None, None),
    )
    return jax.shard_map(
        local,
        mesh=mesh,
        in_specs=placed,
        out_specs=(
            P(("dp", "expert"), None),
            P("expert", "dp", None),
            P("expert", "dp", None),
            P("expert", "dp", None),
        ),
        check_vma=False,
    )
```

profile of v0, /device:TPU:1, one launch (start us, length us, event | category | flops | bytes accessed | tf_op | source)
XLA Modules:
  0.0 227.5 jit_solution(13058739347543928477)
XLA Ops:
  14.1 3.9 %reshape.108 = bf16[512,2048]{1,0:T(8,128)(2,1)} reshape(bf16[128,4,2048]{2,1,0:T(4,128)(2,1)} %broadcast_in_dim.20) | data formatting | bytes 4194304 | tf_op jit(solution)/shard_map/reshape | solution.py:43
  18.2 6.5 %scatter_custom_fusion.1 = bf16[640,2048]{1,0:T(8,128)(2,1)} fusion(s32[512]{0:T(512)S(1)} %bitcast.62, bf16[512,2048]{1,0:T(8,128)(2,1)} %reshape.108, bf16[]{:T(256)} %constant.5.clone.1), kind=kCustom, calls=%fused_computation.25 | custom fusion | bytes 2621952 | tf_op jit(solution)/shard_map/scatter | solution.py:47
  24.7 7.8 %all-to-all-start.1 = ((bf16[16,40,2048]{2,1,0:T(8,128)(2,1)}), bf16[16,40,2048]{2,1,0:T(8,128)(2,1)}, u32[]{:S(2)}, u32[]{:S(2)}) async-start(bf16[16,40,2048]{2,1,0:T(8,128)(2,1)} %bitcast.60), calls=%async_computation.1 | async-start | bytes 5242880 | tf_op jit(solution)/shard_map/all_to_all | solution.py:50
  35.5 5.3 %convert_element_type.39 = f32[512,2048]{1,0:T(8,128)} reshape(f32[128,4,2048]{2,1,0:T(4,128)} %broadcast_in_dim.19) | data formatting | bytes 8388608 | tf_op jit(solution)/shard_map/convert_element_type | solution.py:45
  41.0 7.1 %scatter_custom_fusion = bf16[640,2048]{1,0:T(8,128)(2,1)} fusion(s32[512]{0:T(512)S(1)} %bitcast.63, f32[512,2048]{1,0:T(8,128)} %convert_element_type.39, f32[512]{0:T(512)S(1)} %mul.54, bf16[]{:T(256)} %constant.5.clone.1), kind=kCustom, calls=%fused_computation.18 | custom fusion | flops 2097152 | bytes 6817794 | tf_op jit(solution)/shard_map/scatter | solution.py:48
  48.1 23.3 %all-to-all-done.1 = bf16[16,40,2048]{2,1,0:T(8,128)(2,1)} async-done(((bf16[16,40,2048]{2,1,0:T(8,128)(2,1)}), bf16[16,40,2048]{2,1,0:T(8,128)(2,1)}, u32[]{:S(2)}, u32[]{:S(2)}) %all-to-all-start.1) | async-done | bytes 2621472 | tf_op jit(solution)/shard_map/all_to_all | solution.py:50
  71.4 4.5 %all-to-all-start = ((bf16[16,40,2048]{2,1,0:T(8,128)(2,1)}), bf16[16,40,2048]{2,1,0:T(8,128)(2,1)}, u32[]{:S(2)}, u32[]{:S(2)}) async-start(bf16[16,40,2048]{2,1,0:T(8,128)(2,1)} %bitcast.59), calls=%async_computation | async-start | bytes 5242880 | tf_op jit(solution)/shard_map/all_to_all | solution.py:57
  76.1 5.6 %fusion.2 = f32[640,704]{0,1:T(8,128)} fusion(bf16[640,2048]{1,0:T(8,128)(2,1)} %bitcast.7, bf16[1,2048,704]{1,2,0:T(8,128)(2,1)S(1)} %copy-done), kind=kOutput, calls=%fused_computation.11 | convolution fusion | flops 1845493760 | bytes 7307264 | tf_op jit(solution)/shard_map/dot_general | solution.py:8
  81.7 5.4 %fusion.5 = f32[640,704]{0,1:T(8,128)} fusion(bf16[640,2048]{1,0:T(8,128)(2,1)} %bitcast.7, bf16[1,2048,704]{1,2,0:T(8,128)(2,1)S(1)} %copy-done.5), kind=kOutput, calls=%fused_computation.14 | convolution fusion | flops 1845493760 | bytes 7307264 | tf_op jit(solution)/shard_map/dot_general | solution.py:9
  87.1 24.6 %all-to-all-done = bf16[16,40,2048]{2,1,0:T(8,128)(2,1)} async-done(((bf16[16,40,2048]{2,1,0:T(8,128)(2,1)}), bf16[16,40,2048]{2,1,0:T(8,128)(2,1)}, u32[]{:S(2)}, u32[]{:S(2)}) %all-to-all-start) | async-done | bytes 2621472 | tf_op jit(solution)/shard_map/all_to_all | solution.py:57
  111.8 5.4 %convolution_convert_fusion = bf16[2048,704]{0,1:T(8,128)(2,1)S(1)} fusion(bf16[640,2048]{1,0:T(8,128)(2,1)} %bitcast.4, f32[640,704]{0,1:T(8,128)} %fusion.5, f32[640,704]{0,1:T(8,128)} %fusion.2), kind=kOutput, calls=%fused_computation.6 | convolution fusion | flops 1849638912 | bytes 9109504 | tf_op jit(solution)/shard_map/dot_general | solution.py:27
  117.2 4.5 %multiply_convert_fusion.3 = (bf16[640,704]{0,1:T(8,128)(2,1)S(1)}, bf16[640,704]{0,1:T(8,128)(2,1)S(1)}) fusion(f32[640,704]{0,1:T(8,128)S(1)} %copy-done.7, f32[640,704]{0,1:T(8,128)S(1)} %copy-done.8, bf16[640,2048]{1,0:T(8,128)(2,1)} %bitcast.4, bf16[1,2048,704]{1,2,0:T(8,128)(2,1)S(1)} %copy-done.4), kind=kOutput, calls=%fused_computation.21 | convolution fusion | flops 1851351040 | bytes 10911744 | tf_op jit(solution)/shard_map/dot_general | solution.py:13
  121.7 4.8 %convolution_convert_fusion.1 = bf16[2048,704]{0,1:T(8,128)(2,1)S(1)} fusion(bf16[640,704]{0,1:T(8,128)(2,1)S(1)} %get-tuple-element.4, bf16[640,2048]{1,0:T(8,128)(2,1)} %bitcast.7), kind=kOutput, calls=%fused_computation.7 | convolution fusion | flops 1846935552 | bytes 6406144 | tf_op jit(solution)/shard_map/dot_general | solution.py:26
  126.6 4.2 %convolution_convert_fusion.2 = bf16[2048,704]{0,1:T(8,128)(2,1)S(1)} fusion(bf16[640,704]{0,1:T(8,128)(2,1)S(1)} %get-tuple-element.5, bf16[640,2048]{1,0:T(8,128)(2,1)} %bitcast.7), kind=kOutput, calls=%fused_computation.8 | convolution fusion | flops 1846935552 | bytes 6406144 | tf_op jit(solution)/shard_map/dot_general | solution.py:25
  130.7 4.4 %pad_maximum_fusion = bf16[2048,2112]{0,1:T(8,128)(2,1)} fusion(bf16[2048,704]{0,1:T(8,128)(2,1)S(1)} %convolution_convert_fusion, bf16[2048,704]{0,1:T(8,128)(2,1)S(1)} %convolution_convert_fusion.1, bf16[2048,704]{0,1:T(8,128)(2,1)S(1)} %convolution_convert_fusion.2), kind=kLoop, calls=%fused_computation.3 | loop fusion | flops 25952256 | bytes 17301504 | tf_op jit(solution)/shard_map/concatenate | solution.py:28
  135.1 11.6 %copy.21 = bf16[2048,2112]{1,0:T(8,128)(2,1)} copy(bf16[2048,2112]{0,1:T(8,128)(2,1)} %pad_maximum_fusion) | data formatting | bytes 17301504
  146.8 3.6 %fusion = f32[640,2048]{1,0:T(8,128)S(1)} fusion(bf16[640,704]{0,1:T(8,128)(2,1)} %copy-done.1, bf16[1,2048,704]{1,2,0:T(8,128)(2,1)S(1)} %copy-done), kind=kOutput, calls=%fused_computation.9 | convolution fusion | flops 1845493760 | bytes 9027584 | tf_op jit(solution)/shard_map/dot_general | solution.py:16
  150.4 3.8 %add_convert_fusion = bf16[640,2048]{1,0:T(8,128)(2,1)} fusion(f32[640,2048]{1,0:T(8,128)S(1)} %fusion, bf16[640,704]{0,1:T(8,128)(2,1)S(1)} %copy-done.10, bf16[1,2048,704]{1,2,0:T(8,128)(2,1)S(1)} %copy-done.6), kind=kOutput, calls=%fused_computation.4 | convolution fusion | flops 1848115200 | bytes 11649024 | tf_op jit(solution)/shard_map/dot_general | solution.py:17
  154.2 5.1 %all-to-all-start.2 = ((bf16[16,40,2048]{2,1,0:T(8,128)(2,1)}), bf16[16,40,2048]{2,1,0:T(8,128)(2,1)}, u32[]{:S(2)}, u32[]{:S(2)}) async-start(bf16[16,40,2048]{2,1,0:T(8,128)(2,1)} %bitcast.61), calls=%async_computation.2 | async-start | bytes 5242880 | tf_op jit(solution)/shard_map/all_to_all | solution.py:68
  159.3 34.1 %all-to-all-done.2 = bf16[16,40,2048]{2,1,0:T(8,128)(2,1)} async-done(((bf16[16,40,2048]{2,1,0:T(8,128)(2,1)}), bf16[16,40,2048]{2,1,0:T(8,128)(2,1)}, u32[]{:S(2)}, u32[]{:S(2)}) %all-to-all-start.2) | async-done | bytes 2621472 | tf_op jit(solution)/shard_map/all_to_all | solution.py:68
  193.4 7.4 %gather_fusion = bf16[512,2048]{1,0:T(8,128)(2,1)} fusion(bf16[640,2048]{1,0:T(8,128)(2,1)} %bitcast.11, s32[1024]{0:T(1024)S(1)} %pad_clamp_fusion), kind=kCustom, calls=%fused_computation | custom fusion | bytes 4196352 | tf_op jit(solution)/shard_map/gather | solution.py:71
  200.8 4.2 %gather.6 = bf16[128,4,2048]{2,1,0:T(4,128)(2,1)} reshape(bf16[512,2048]{1,0:T(8,128)(2,1)} %gather_fusion) | data formatting | bytes 4194304 | tf_op jit(solution)/shard_map/gather | solution.py:71
  205.0 5.0 %reduce_sum.25 = bf16[128,2048]{1,0:T(8,128)(2,1)} reduce(bf16[128,4,2048]{2,1,0:T(4,128)(2,1)} %gather.6, bf16[]{:T(256)} %constant.5.clone.1), dimensions={1}, to_apply=%region_5.6 | reduce | flops 786432 | bytes 2621442 | tf_op jit(solution)/shard_map/reduce_sum | solution.py:72
  210.0 8.2 %reduce-scatter.4.cloned.1.call-done = bf16[128,2112]{1,0:T(8,128)(2,1)} async-done(((bf16[2048,2112]{1,0:T(8,128)(2,1)}), bf16[128,2112]{1,0:T(8,128)(2,1)}) %reduce-scatter.4.cloned.1.call-update) | async-done | bytes 540688
  (45 shorter events, 13.0 us)
Async XLA Ops:
  7.2 68.9 %copy-start = (bf16[1,2048,704]{1,2,0:T(8,128)(2,1)S(1)}, bf16[1,2048,704]{1,2,0:T(8,128)(2,1)}, u32[]{:S(2)}) copy-start(bf16[1,2048,704]{1,2,0:T(8,128)(2,1)} %param.11) | copy-start | bytes 8650756
  24.7 7.8 %copy-start.2 = (bf16[128,2048]{1,0:T(8,128)(2,1)S(1)}, bf16[128,2048]{1,0:T(8,128)(2,1)}, u32[]{:S(2)}) copy-start(bf16[128,2048]{1,0:T(8,128)(2,1)} %param.8) | copy-start | bytes 1572868
  24.7 46.7 %all-to-all-start.1 = ((bf16[16,40,2048]{2,1,0:T(8,128)(2,1)}), bf16[16,40,2048]{2,1,0:T(8,128)(2,1)}, u32[]{:S(2)}, u32[]{:S(2)}) async-start(bf16[16,40,2048]{2,1,0:T(8,128)(2,1)} %bitcast.60), calls=%async_computation.1 | async-start | bytes 5242880 | tf_op jit(solution)/shard_map/all_to_all | solution.py:50
  35.5 5.3 %copy-start.3 = (f32[128,4]{0,1:T(4,128)S(1)}, f32[128,4]{0,1:T(4,128)}, u32[]{:S(2)}) copy-start(f32[128,4]{0,1:T(4,128)} %param.10) | copy-start | bytes 6148
  71.4 40.3 %all-to-all-start = ((bf16[16,40,2048]{2,1,0:T(8,128)(2,1)}), bf16[16,40,2048]{2,1,0:T(8,128)(2,1)}, u32[]{:S(2)}, u32[]{:S(2)}) async-start(bf16[16,40,2048]{2,1,0:T(8,128)(2,1)} %bitcast.59), calls=%async_computation | async-start | bytes 5242880 | tf_op jit(solution)/shard_map/all_to_all | solution.py:57
  75.9 142.4 %reduce-scatter.4.cloned.1.call-start = ((), (), s32[]{:S(2)}) async-start(), calls=%async_computation.4 | async-start | bytes 9469952
  76.1 5.6 %copy-start.5 = (bf16[1,2048,704]{1,2,0:T(8,128)(2,1)S(1)}, bf16[1,2048,704]{1,2,0:T(8,128)(2,1)}, u32[]{:S(2)}) copy-start(bf16[1,2048,704]{1,2,0:T(8,128)(2,1)} %param.12) | copy-start | bytes 8650756
  111.7 5.4 %copy-start.4 = (bf16[1,2048,704]{1,2,0:T(8,128)(2,1)S(1)}, bf16[1,2048,704]{1,2,0:T(8,128)(2,1)}, u32[]{:S(2)}) copy-start(bf16[1,2048,704]{1,2,0:T(8,128)(2,1)} %param.13) | copy-start | bytes 8650756
  111.7 5.4 %copy-start.7 = (f32[640,704]{0,1:T(8,128)S(1)}, f32[640,704]{0,1:T(8,128)}, u32[]{:S(2)}) copy-start(f32[640,704]{0,1:T(8,128)} %fusion.2) | copy-start | bytes 5406724
  111.7 5.4 %copy-start.8 = (f32[640,704]{0,1:T(8,128)S(1)}, f32[640,704]{0,1:T(8,128)}, u32[]{:S(2)}) copy-start(f32[640,704]{0,1:T(8,128)} %fusion.5) | copy-start | bytes 5406724
  121.7 4.8 %copy-start.9 = (bf16[640,704]{0,1:T(8,128)(2,1)}, bf16[640,704]{0,1:T(8,128)(2,1)S(1)}, u32[]{:S(2)}) copy-start(bf16[640,704]{0,1:T(8,128)(2,1)S(1)} %get-tuple-element.4) | copy-start | bytes 2703364
  121.7 4.8 %copy-start.1 = (bf16[640,704]{0,1:T(8,128)(2,1)}, bf16[640,704]{0,1:T(8,128)(2,1)S(1)}, u32[]{:S(2)}) copy-start(bf16[640,704]{0,1:T(8,128)(2,1)S(1)} %get-tuple-element.5) | copy-start | bytes 2703364
  146.8 3.6 %copy-start.6 = (bf16[1,2048,704]{1,2,0:T(8,128)(2,1)S(1)}, bf16[1,2048,704]{1,2,0:T(8,128)(2,1)}, u32[]{:S(2)}) copy-start(bf16[1,2048,704]{1,2,0:T(8,128)(2,1)} %param.12) | copy-start | bytes 8650756
  146.8 3.6 %copy-start.10 = (bf16[640,704]{0,1:T(8,128)(2,1)S(1)}, bf16[640,704]{0,1:T(8,128)(2,1)}, u32[]{:S(2)}) copy-start(bf16[640,704]{0,1:T(8,128)(2,1)} %copy-done.9) | copy-start | bytes 2703364
  154.2 39.2 %all-to-all-start.2 = ((bf16[16,40,2048]{2,1,0:T(8,128)(2,1)}), bf16[16,40,2048]{2,1,0:T(8,128)(2,1)}, u32[]{:S(2)}, u32[]{:S(2)}) async-start(bf16[16,40,2048]{2,1,0:T(8,128)(2,1)} %bitcast.61), calls=%async_computation.2 | async-start | bytes 5242880 | tf_op jit(solution)/shard_map/all_to_all | solution.py:68
Sparse Core Ops, SparseCore 0:
  146.9 71.3 reduce-scatter.3
where the time goes:
time: 231 us; the launch traced here: 228 us
  waiting for transfers between devices  90.2 us (39%)
  local copies, waits for them, and re-layouts  49.5 us (21%)
  matrix products  37.3 us (16%)
  other arithmetic  18.7 us (8%)
  starting transfers between devices  17.5 us (8%)
  between operations  14.3 us (6%)
    all_to_all x1, waiting for transfers between devices, local(): lax.all_to_all(back.reshape(groups, capacity, width), 'expert', split_axi...  34.1 us
    all_to_all x1, waiting for transfers between devices, local(): lax.all_to_all(send_cot.reshape(groups, capacity, width), 'expert', split...  24.6 us
    all_to_all x1, waiting for transfers between devices, local(): lax.all_to_all(send_in.reshape(groups, capacity, width), 'expert', split_...  23.3 us
    unnamed x26, local copies, waits for them, and re-layouts  14 us
    gather x2, local copies, waits for them, and re-layouts, local(): returned.reshape(groups * capacity, width)[position].astype(jnp.float32)  11.6 us
    unnamed x2, waiting for transfers between devices  8.22 us
    all_to_all x1, starting transfers between devices, local(): lax.all_to_all(send_in.reshape(groups, capacity, width), 'expert', split_...  7.76 us
    scatter x1, other arithmetic, local(): jnp.zeros((groups * capacity, width), jnp.bfloat16).at[position].set(scaled)  7.12 us
  transfers between devices with their start and end apart: 4, of which 4 were waited for; matrix products, arithmetic and copies ran while one was open for 22% of the time, Pallas kernels for 0%

commit v1 on v0

v1 whole, which is shorter than its diff:
```python
import jax
import jax.numpy as jnp
from jax import lax
from jax.experimental import pallas as pl
from jax.experimental.pallas import tpu as pltpu
from jax.sharding import PartitionSpec as P

MESH = pl.DeviceIdType.MESH
BF = jnp.bfloat16
F32 = jnp.float32
TOK, WID, HID, CAP, NEXP = 128, 2048, 704, 40, 16
FB = 256
ROWS = 4 * CAP
ALL = 4 * ROWS
NN = (((1,), (0,)), ((), ()))
NT = (((1,), (1,)), ((), ()))
TN = (((0,), (0,)), ((), ()))


def dot(a, b, dims=NN):
    return lax.dot_general(a, b, dims, preferred_element_type=F32)


def kernel(
    tok_hbm, go_hbm, routes_ref, comb_ref, wg_hbm, wu_hbm, wd_hbm,
    out_tok, out_g, out_u, out_d,
    wg, wu, wd, meta, pmat, crow, tbuf, gbuf, tsend, ssend, xin, sin,
    gate, upper, gh, hidden, gg, gu, mine, csend, crecv, zsend, zrecv, brecv,
    wsem, lsem, ms, mr, ags, agr, a2s, a2r, cs, cr, zs, zr, bs, br, ps, pr,
):
    e = lax.axis_index("expert")
    d = lax.axis_index("dp")
    x, y, z, c = lax.rem(e, 4), e // 4, d // 2, lax.rem(d, 2)

    def along_y(r):
        return (d, lax.rem(y + r, 4) * 4 + x)

    def along_x(r):
        return (d, y * 4 + lax.rem(x + r, 4))

    def along_z(r):
        return (lax.rem(z + r + 8, 8) * 2 + c, e)

    other_core = (z * 2 + 1 - c, e)
    spread = (along_y, along_x)
    route = (along_x, along_y)

    def block(h, i):
        if h == 0:
            return lax.rem(z + 4 - i, 8)
        return lax.rem(z + 4 + i, 8) if i else z

    def remote(src, dst, ss, rs, dev):
        return pltpu.make_async_remote_copy(
            src_ref=src, dst_ref=dst, send_sem=ss, recv_sem=rs, device_id=dev, device_id_type=MESH
        )

    arrays = ((tok_hbm, tbuf), (go_hbm, gbuf))

    def load(a, h, i):
        cols = pl.ds(pl.multiple_of(block(h, i) * FB, FB), FB)
        return pltpu.make_async_copy(
            arrays[a][0].at[:, cols], arrays[a][1].at[h, i, pl.ds(0, TOK)], lsem.at[a, h, i]
        )

    for a in range(2):
        for i in range(4):
            for h in range(2):
                load(a, h, i).start()
    for m, (src, dst) in enumerate(((wg_hbm, wg), (wu_hbm, wu), (wd_hbm, wd))):
        for h in range(2):
            for i in range(4):
                rows = pl.ds(pl.multiple_of(block(h, i) * FB, FB), FB)
                pltpu.make_async_copy(
                    src.at[0, rows], dst.at[h, pl.ds(i * FB, FB)], wsem.at[m, h, i]
                ).start()

    def wait_weights(m):
        src, dst = ((wg_hbm, wg), (wu_hbm, wu), (wd_hbm, wd))[m]
        for h in range(2):
            for i in range(4):
                pltpu.make_async_copy(
                    src.at[0, pl.ds(0, FB)], dst.at[h, pl.ds(i * FB, FB)], wsem.at[m, h, i]
                ).wait()

    barrier = pltpu.get_barrier_semaphore()
    peers = [f(r) for f in (along_x, along_y) for r in (1, 2, 3)] + [along_z(1), along_z(-1), other_core]
    for dev in peers:
        pl.semaphore_signal(barrier, inc=1, device_id=dev, device_id_type=MESH)

    experts = lax.broadcasted_iota(jnp.int32, (TOK, 128), 1)
    taken = jnp.zeros((TOK, 128), F32)
    weight = jnp.zeros((TOK, 128), F32)
    for k in range(4):
        hit = routes_ref[:, k : k + 1] == experts
        taken = taken + jnp.where(hit, 1.0, 0.0)
        weight = weight + jnp.where(hit, comb_ref[:, k : k + 1], 0.0)
    earlier = (
        lax.broadcasted_iota(jnp.int32, (TOK, TOK), 0) > lax.broadcasted_iota(jnp.int32, (TOK, TOK), 1)
    ).astype(BF)
    slot = dot(earlier, taken.astype(BF))
    key = jnp.where(taken > 0.5, slot, -10000.0)
    for h in range(2):
        meta[h, 0, 0:NEXP, :] = key.T[0:NEXP]
        meta[h, 0, NEXP : 2 * NEXP, :] = weight.T[0:NEXP]

    pl.semaphore_wait(barrier, len(peers))

    for h in range(2):
        for r in (1, 2, 3):
            remote(meta.at[h, 0], meta.at[h, 4 - r], ms.at[h], mr.at[h], spread[h](r)).start()

    def gather_send(a, h, i):
        buf = arrays[a][1]
        for r in (1, 3, 2):
            remote(
                buf.at[h, i, pl.ds(0, TOK)],
                buf.at[h, i, pl.ds((4 - r) * TOK, TOK)],
                ags.at[a, h, i],
                agr.at[a, h, i],
                spread[h](r),
            ).start()

    def gather_all(a, h, i):
        part = arrays[a][1].at[h, i, pl.ds(TOK, 3 * TOK)]
        return remote(part, part, ags.at[a, h, i], agr.at[a, h, i], spread[h](1))

    for i in range(4):
        for h in range(2):
            load(0, h, i).wait()
            gather_send(0, h, i)

    for h in range(2):
        m = meta.at[h, pl.ds(1, 3)]
        remote(m, m, ms.at[h], mr.at[h], spread[h](1)).wait()
        for r in range(4):
            ex = route[h](r)[1]
            keys = jnp.concatenate([meta[h, s, pl.ds(ex, 1), :] + float(s * CAP) for s in range(4)], axis=1)
            wts = jnp.concatenate([meta[h, s, pl.ds(ex + NEXP, 1), :] for s in range(4)], axis=1)
            hit = lax.broadcasted_iota(jnp.int32, (ROWS, 4 * TOK), 0).astype(F32) == keys
            pmat[h, r * ROWS : (r + 1) * ROWS, :] = jnp.where(hit, 1.0, 0.0).astype(BF)
            crow[h, r * ROWS : (r + 1) * ROWS, :] = jnp.sum(jnp.where(hit, wts, 0.0), axis=1, keepdims=True)

    def second_send(a, h, i):
        snd, dst = ((tsend, xin), (ssend, sin))[a]
        for r in (2, 1, 3):
            remote(
                snd.at[h, i, pl.ds(r * ROWS, ROWS)],
                dst.at[h, i, pl.ds((4 - r) * ROWS, ROWS)],
                a2s.at[a, h, i],
                a2r.at[a, h, i],
                route[h](r),
            ).start()

    def second_all(a, h, i):
        snd, dst = ((tsend, xin), (ssend, sin))[a]
        return remote(
            snd.at[h, i, pl.ds(ROWS, 3 * ROWS)],
            dst.at[h, i, pl.ds(ROWS, 3 * ROWS)],
            a2s.at[a, h, i],
            a2r.at[a, h, i],
            route[h](1),
        )

    for i in range(4):
        for h in range(2):
            gather_all(0, h, i).wait_recv()
            rows = dot(pmat[h], tbuf[h, i]).astype(BF)
            xin[h, i, 0:ROWS, :] = rows[0:ROWS]
            tsend[h, i] = rows
            second_send(0, h, i)
            load(1, h, i).wait()
            gather_send(1, h, i)

    for i in range(4):
        for h in range(2):
            gather_all(1, h, i).wait_recv()
            rows = (dot(pmat[h], gbuf[h, i]) * crow[h]).astype(BF)
            sin[h, i, 0:ROWS, :] = rows[0:ROWS]
            ssend[h, i] = rows
            second_send(1, h, i)

    wait_weights(0)
    wait_weights(1)

    def project(src, w, h, rows):
        total = dot(src[h, 0, rows, :], w[h, 0:FB, :])
        for i in range(1, 4):
            total = total + dot(src[h, i, rows, :], w[h, i * FB : (i + 1) * FB, :])
        return total

    def add_other(acc, val, r):
        for s in range(4):
            at = pl.ds(pl.multiple_of(s * ROWS + r * CAP, 8), CAP)
            acc[at, :] = acc[at, :] + val[s * CAP : (s + 1) * CAP]

    def other_order(acc, r):
        return jnp.concatenate(
            [acc[pl.ds(pl.multiple_of(s * ROWS + r * CAP, 8), CAP), :] for s in range(4)], axis=0
        )

    def tile(r):
        return pl.ds(pl.multiple_of(r * ROWS, ROWS), ROWS)

    for i in range(4):
        second_all(0, 0, i).wait_recv()

    @pl.loop(0, 4)
    def _(r):
        gate[tile(r), :] = project(xin, wg, 0, tile(r))
        upper[tile(r), :] = project(xin, wu, 0, tile(r))

    for i in range(4):
        second_all(0, 1, i).wait_recv()

    @pl.loop(0, 4)
    def _(r):
        add_other(gate, project(xin, wg, 1, tile(r)), r)
        add_other(upper, project(xin, wu, 1, tile(r)), r)

    @pl.loop(0, 4)
    def _(r):
        g, u = gate[tile(r), :], upper[tile(r), :]
        s = jax.nn.sigmoid(g)
        active = g * s
        hid = active * u
        hidden[0, tile(r), :] = hid.astype(BF)
        gh[tile(r), :] = hid
        gate[tile(r), :] = u * s * (1.0 + g * (1.0 - s))
        upper[tile(r), :] = active

    @pl.loop(0, 4)
    def _(r):
        hidden[1, tile(r), :] = other_order(gh, r).astype(BF)

    outs = (out_d, out_g, out_u)

    def partial(m, h, i, rows_ref, factor):
        val = dot(rows_ref[h, i], factor[h], TN)
        low, high = val[0:TOK], val[TOK : 2 * TOK]
        own = jnp.where(c == 0, low, high)
        if h == 1 and i == 0:
            outs[m][0] = own
        else:
            mine[m, h] = own
        csend[m, h] = jnp.where(c == 0, high, low).astype(BF)
        remote(csend.at[m, h], crecv.at[m, h, i], cs.at[m, h, i], cr.at[m, h, i], other_core).start()

    def swapped(m, h, i):
        remote(csend.at[m, h], crecv.at[m, h, i], cs.at[m, h, i], cr.at[m, h, i], other_core).wait()

    def zcopy(m, h, i, rows=pl.ds(0, TOK)):
        return remote(
            zsend.at[m, h, i % 2, rows],
            zrecv.at[m, h, i, rows],
            zs.at[m, h, i],
            zr.at[m, h, i],
            along_z(1 if h == 0 else -1),
        )

    halves = (pl.ds(0, 64), pl.ds(64, 64))

    def forward(m, i):
        if i == 0:
            swapped(m, 0, 0)
            val = (mine[m, 0] + crecv[m, 0, 0].astype(F32)).astype(BF)
            for h in range(2):
                zsend[m, h, 0, halves[h], :] = val[64 * h : 64 * h + 64]
                zcopy(m, h, 0, halves[h]).start()
            swapped(m, 1, 0)
            outs[m][0] = outs[m][0] + crecv[m, 1, 0].astype(F32)
            return
        for h in range(2):
            swapped(m, h, i)
            if i == 1:
                zcopy(m, h, 0, halves[h]).wait_recv()
                val = mine[m, h] + crecv[m, h, 1].astype(F32)
                got = zrecv[m, h, 0, halves[h], :].astype(F32)
                keep = val[64 * (1 - h) : 64 * (1 - h) + 64]
                zsend[m, h, 1, halves[h], :] = (val[64 * h : 64 * h + 64] + got).astype(BF)
                zsend[m, h, 1, halves[1 - h], :] = keep.astype(BF)
            else:
                zcopy(m, h, i - 1).wait_recv()
                if i == 2:
                    zcopy(m, h, 0, halves[h]).wait_send()
                else:
                    zcopy(m, h, i - 2).wait_send()
                val = mine[m, h] + crecv[m, h, i].astype(F32) + zrecv[m, h, i - 1].astype(F32)
                zsend[m, h, i % 2] = val.astype(BF)
            zcopy(m, h, i).start()

    def settle(m):
        for h in range(2):
            zcopy(m, h, 3).wait_recv()
            zcopy(m, h, 2).wait_send()
            zcopy(m, h, 3).wait_send()
        outs[m][0] = outs[m][0] + (zrecv[m, 0, 3].astype(F32) + zrecv[m, 1, 3].astype(F32))

    for i in range(4):
        for h in range(2):
            second_all(1, h, i).wait_recv()
            partial(0, h, i, sin, hidden)
        forward(0, i)

    wait_weights(2)

    @pl.loop(0, 4)
    def _(r):
        gh[tile(r), :] = project(sin, wd, 0, tile(r))

    @pl.loop(0, 4)
    def _(r):
        add_other(gh, project(sin, wd, 1, tile(r)), r)

    @pl.loop(0, 4)
    def _(r):
        v = gh[tile(r), :]
        a = v * gate[tile(r), :]
        b = v * upper[tile(r), :]
        gate[tile(r), :] = a
        upper[tile(r), :] = b
        gg[0, tile(r), :] = a.astype(BF)
        gu[0, tile(r), :] = b.astype(BF)

    @pl.loop(0, 4)
    def _(r):
        gg[1, tile(r), :] = other_order(gate, r).astype(BF)
        gu[1, tile(r), :] = other_order(upper, r).astype(BF)

    def back_copy(h, i, r):
        return remote(
            tsend.at[h, i, pl.ds(r * ROWS, ROWS)],
            brecv.at[h, i, pl.ds((4 - r) * ROWS, ROWS)],
            bs.at[h, i],
            br.at[h, i],
            route[h](r),
        )

    def back_all(h, i):
        return remote(
            tsend.at[h, i, pl.ds(ROWS, 3 * ROWS)],
            brecv.at[h, i, pl.ds(ROWS, 3 * ROWS)],
            bs.at[h, i],
            br.at[h, i],
            route[h](1),
        )

    def back(h, i):
        at = slice(i * FB, (i + 1) * FB)
        second_all(0, h, i).wait_send()
        val = (dot(gg[h], wg[h, at, :], NT) + dot(gu[h], wu[h, at, :], NT)).astype(BF)
        brecv[h, i, 0:ROWS, :] = val[0:ROWS]
        tsend[h, i] = val
        for r in (2, 1, 3):
            back_copy(h, i, r).start()

    def home_all(h, i):
        return remote(
            ssend.at[h, i, pl.ds(TOK, 3 * TOK)],
            tbuf.at[h, i, pl.ds(TOK, 3 * TOK)],
            ps.at[h, i],
            pr.at[h, i],
            spread[h](1),
        )

    def home(h, i):
        back_all(h, i).wait_recv()
        second_all(1, h, i).wait_send()
        gather_all(0, h, i).wait_send()
        val = dot(pmat[h], brecv[h, i], TN).astype(BF)
        tbuf[h, i, 0:TOK, :] = val[0:TOK]
        ssend[h, i, 0 : 4 * TOK, :] = val
        for s in (1, 3, 2):
            remote(
                ssend.at[h, i, pl.ds(s * TOK, TOK)],
                tbuf.at[h, i, pl.ds((4 - s) * TOK, TOK)],
                ps.at[h, i],
                pr.at[h, i],
                spread[h](s),
            ).start()

    def finish(h, i):
        home_all(h, i).wait_recv()
        total = tbuf[h, i, 0:TOK, :].astype(F32)
        for s in range(1, 4):
            total = total + tbuf[h, i, s * TOK : (s + 1) * TOK, :].astype(F32)
        cols = pl.ds(pl.multiple_of(block(h, i) * FB, FB), FB)
        out_tok[:, cols] = total.astype(BF)

    def partials(i):
        for h in range(2):
            partial(1, h, i, xin, gg)
            partial(2, h, i, xin, gu)

    def both(f, i):
        f(0, i)
        f(1, i)

    partials(0)
    both(back, 0)
    forward(1, 0)
    forward(2, 0)
    settle(0)
    for i in (1, 2, 3):
        both(back, i)
    partials(1)
    both(home, 0)
    both(home, 1)
    forward(1, 1)
    forward(2, 1)
    partials(2)
    both(home, 2)
    both(home, 3)
    both(finish, 0)
    forward(1, 2)
    forward(2, 2)
    partials(3)
    for i in (1, 2, 3):
        both(finish, i)
    forward(1, 3)
    forward(2, 3)
    settle(1)
    settle(2)

    for h in range(2):
        for i in range(4):
            gather_all(1, h, i).wait_send()
            back_all(h, i).wait_send()
            home_all(h, i).wait_send()


def local(tokens, grad_out, routes, combine, w_gate, w_up, w_down):
    vm = pl.BlockSpec(memory_space=pltpu.VMEM)
    hbm = pl.BlockSpec(memory_space=pl.ANY)
    grad = jax.ShapeDtypeStruct((1, TOK, HID), F32)
    sem = pltpu.SemaphoreType.DMA
    V = pltpu.VMEM
    return pl.pallas_call(
        kernel,
        name="experts",
        out_shape=(jax.ShapeDtypeStruct((TOK, WID), BF), grad, grad, grad),
        in_specs=[hbm, hbm, vm, vm, hbm, hbm, hbm],
        out_specs=(vm, vm, vm, vm),
        scratch_shapes=[
            V((2, 1024, HID), BF), V((2, 1024, HID), BF), V((2, 1024, HID), BF),
            V((2, 4, 2 * NEXP, 128), F32),
            V((2, ALL, 4 * TOK), BF),
            V((2, ALL, 1), F32),
            V((2, 4, 4 * TOK, FB), BF), V((2, 4, 4 * TOK, FB), BF),
            V((2, 4, ALL, FB), BF), V((2, 4, ALL, FB), BF),
            V((2, 4, ALL, FB), BF), V((2, 4, ALL, FB), BF),
            V((ALL, HID), F32), V((ALL, HID), F32), V((ALL, HID), F32),
            V((2, ALL, HID), BF), V((2, ALL, HID), BF), V((2, ALL, HID), BF),
            V((3, 2, TOK, HID), F32),
            V((3, 2, TOK, HID), BF),
            V((3, 2, 4, TOK, HID), BF),
            V((3, 2, 2, TOK, HID), BF),
            V((3, 2, 4, TOK, HID), BF),
            V((2, 4, ALL, FB), BF),
            sem((3, 2, 4)), sem((2, 2, 4)), sem((2,)), sem((2,)),
            sem((2, 2, 4)), sem((2, 2, 4)), sem((2, 2, 4)), sem((2, 2, 4)),
            sem((3, 2, 4)), sem((3, 2, 4)), sem((3, 2, 4)), sem((3, 2, 4)),
            sem((2, 4)), sem((2, 4)), sem((2, 4)), sem((2, 4)),
        ],
        compiler_params=pltpu.CompilerParams(
            collective_id=0, has_side_effects=True, vmem_limit_bytes=62 * 2**20
        ),
        cost_estimate=pl.CostEstimate(flops=15 * 10**9, bytes_accessed=12 * 10**6, transcendentals=450560),
    )(tokens, grad_out, routes, combine, w_gate, w_up, w_down)


def solution(mesh):
    rows = P(("dp", "expert"), None)
    weights = P("expert", None, None)
    grads = P("expert", "dp", None)
    return jax.shard_map(
        local,
        mesh=mesh,
        in_specs=(rows, rows, rows, rows, weights, weights, weights),
        out_specs=(rows, grads, grads, grads),
        check_vma=False,
    )
```

time: 231 us -> 151 us (0.65); the launches traced: 228 us -> 151 us
  Pallas kernels: 0 us -> 128 us
  waiting for transfers between devices: 90.2 us -> 0 us
  matrix products: 37.3 us -> 0 us
  local copies, waits for them, and re-layouts: 49.5 us -> 22.6 us
  other arithmetic: 18.7 us -> 0 us
  starting transfers between devices: 17.5 us -> 0 us
  between operations: 14.3 us -> 0.65 us
    pallas_call x0 -> x1, Pallas kernels: none -> 128 us  [local(): pl.pallas_call(kernel, name='experts', out_shape=(jax.ShapeDtypeStruct((T...]
    all_to_all x3 -> x0, waiting for transfers between devices: 82 us -> none  [the longest x1 34.1 us: local(): lax.all_to_all(back.reshape(groups, capacity, width), 'expert', split_axi...]
    dot_general x8 -> x0, matrix products: 37.3 us -> none  [the longest x1 5.57 us: expert_terms(): gate = jnp.dot(rows_in, wg, preferred_element_type=jnp.float32)]
    all_to_all x3 -> x0, starting transfers between devices: 17.3 us -> none  [the longest x1 7.76 us: local(): lax.all_to_all(send_in.reshape(groups, capacity, width), 'expert', split_...]
    gather x2 -> x0, local copies, waits for them, and re-layouts: 11.6 us -> none  [local(): returned.reshape(groups * capacity, width)[position].astype(jnp.float32)]
    unnamed x2 -> x0, waiting for transfers between devices: 8.22 us -> none
    broadcast_in_dim x3 -> x0, local copies, waits for them, and re-layouts: 7.41 us -> none  [the longest x1 3.4 us: local(): repeated = jnp.repeat(tokens, choose, axis=0)]
    scatter x1 -> x0, other arithmetic: 7.12 us -> none  [local(): jnp.zeros((groups * capacity, width), jnp.bfloat16).at[position].set(scaled)]
  transfers between devices with their start and end apart: 4 -> 0, of which waited for: 4 -> 0; matrix products, arithmetic and copies ran while one was open for 22% -> 0% of each run, Pallas kernels for 0% -> 0%
where the time goes in v1:
time: 151 us
  Pallas kernels  128 us (85%)
  local copies, waits for them, and re-layouts  22.6 us (15%)
    pallas_call x1, Pallas kernels, local(): pl.pallas_call(kernel, name='experts', out_shape=(jax.ShapeDtypeStruct((T...  128 us
    unnamed x8, local copies, waits for them, and re-layouts  16.9 us
    pallas_call x3, local copies, waits for them, and re-layouts, local(): pl.pallas_call(kernel, name='experts', out_shape=(jax.ShapeDtypeStruct((T...  5.69 us

profile of v1, /device:TPU:1, one launch (start us, length us, event | category | flops | bytes accessed | tf_op | source)
XLA Modules:
  0.0 150.8 jit_solution(515973819619739716)
XLA Ops:
  0.6 0.0 copy-start
  0.6 1.6 %copy.11.routes_ref = s32[128,4]{1,0:T(8,128)} copy(s32[128,4]{0,1:T(4,128)} %param.9) | data formatting | bytes 4096 | tf_op args[2]
  2.2 1.4 copy.12.comb_ref
  3.6 4.6 %copy.13.wg_hbm = bf16[1,2048,704]{2,1,0:T(8,128)(2,1)} copy(bf16[1,2048,704]{1,2,0:T(8,128)(2,1)} %param.11) | data formatting | bytes 5767168 | tf_op args[4]
  8.2 0.0 copy-done
  8.2 2.8 %copy.14.wu_hbm = bf16[1,2048,704]{2,1,0:T(8,128)(2,1)} copy(bf16[1,2048,704]{1,2,0:T(8,128)(2,1)S(1)} %copy-done) | data formatting | bytes 5767168 | tf_op args[5]
  11.0 4.7 %copy.15.wd_hbm = bf16[1,2048,704]{2,1,0:T(8,128)(2,1)} copy(bf16[1,2048,704]{1,2,0:T(8,128)(2,1)} %param.13) | data formatting | bytes 5767168 | tf_op args[6]
  15.7 127.6 %experts.1 = (bf16[128,2048]{1,0:T(8,128)(2,1)}, f32[1,128,704]{2,1,0:T(8,128)}, f32[1,128,704]{2,1,0:T(8,128)}, f32[1,128,704]{2,1,0:T(8,128)}) custom-call(bf16[128,2048]{1,0:T(8,128)(2,1)} %tok_hbm.1, bf16[128,2048]{1,0:T(8,128)(2,1)} %go_hbm.1, s32[128,4]{1,0:T(8,128)} %copy.11.routes_ref, f32[128,4]{1,0:T(8,128)} %copy.12.comb_ref, ...), custom_call_target="tpu_custom_call" | custom-call | flops 15000000512 | bytes 12000000 | tf_op jit(solution)/shard_map/experts/pallas_call | solution.py:438
  143.3 1.9 %copy.16 = f32[1,128,704]{1,2,0:T(8,128)} copy(f32[1,128,704]{2,1,0:T(8,128)} %get-tuple-element.5) | data formatting | bytes 720896 | tf_op jit(solution)/shard_map/experts/pallas_call | solution.py:438
  145.2 1.9 %copy.17 = f32[1,128,704]{1,2,0:T(8,128)} copy(f32[1,128,704]{2,1,0:T(8,128)} %get-tuple-element.6) | data formatting | bytes 720896 | tf_op jit(solution)/shard_map/experts/pallas_call | solution.py:438
  147.1 1.9 %copy.18 = f32[1,128,704]{1,2,0:T(8,128)} copy(f32[1,128,704]{2,1,0:T(8,128)} %get-tuple-element.7) | data formatting | bytes 720896 | tf_op jit(solution)/shard_map/experts/pallas_call | solution.py:438
  149.0 1.9 %copy.20 = bf16[128,2048]{1,0:T(8,128)(2,1)} copy(bf16[128,2048]{1,0:T(8,128)(2,1)} %get-tuple-element.12) | data formatting | bytes 1048576
Async XLA Ops:
  0.6 7.6 %copy-start = (bf16[1,2048,704]{1,2,0:T(8,128)(2,1)S(1)}, bf16[1,2048,704]{1,2,0:T(8,128)(2,1)}, u32[]{:S(2)}) copy-start(bf16[1,2048,704]{1,2,0:T(8,128)(2,1)} %param.12) | copy-start | bytes 8650756

commit v2 on v1

v2 whole, which is shorter than its diff:
```python
import jax
import jax.numpy as jnp
from jax import lax
from jax.experimental import pallas as pl
from jax.experimental.pallas import tpu as pltpu
from jax.sharding import PartitionSpec as P

AHEAD = 3
LOOK, LAG, PASS = 6, 3, True
MESH = pl.DeviceIdType.MESH
BF = jnp.bfloat16
F32 = jnp.float32
TOK, WID, HID, CAP, NEXP = 128, 2048, 704, 40, 16
FB = 256
ROWS = 4 * CAP
ALL = 4 * ROWS
NN = (((1,), (0,)), ((), ()))
NT = (((1,), (1,)), ((), ()))
TN = (((0,), (0,)), ((), ()))


def dot(a, b, dims=NN):
    return lax.dot_general(a, b, dims, preferred_element_type=F32)


def kernel(
    tok_hbm, go_hbm, routes_ref, comb_ref, wg_hbm, wu_hbm, wd_hbm,
    out_tok, out_g, out_u, out_d,
    wg, wu, wd, meta, pmat, pback, crow, tbuf, gbuf, tsend, ssend, xin, sin,
    gate, upper, gh, hidden, ggt, gut, gg, gu, mine, last, csend, crecv, zsend, zrecv, brecv, home_rows,
    wsem, lsem, osem, ms, mr, ags, agr, a2s, a2r, cs, cr, zs, zr, bs, br, ps, pr,
):
    e = lax.axis_index("expert")
    d = lax.axis_index("dp")
    x, y, z, c = lax.rem(e, 4), e // 4, d // 2, lax.rem(d, 2)

    def along_y(r):
        return (d, lax.rem(y + r, 4) * 4 + x)

    def along_x(r):
        return (d, y * 4 + lax.rem(x + r, 4))

    def along_z(r):
        return (lax.rem(z + r + 8, 8) * 2 + c, e)

    other_core = (z * 2 + 1 - c, e)
    spread = (along_y, along_x)
    route = (along_x, along_y)

    def block(h, i):
        if h == 0:
            return lax.rem(z + 4 - i, 8)
        return lax.rem(z + 4 + i, 8) if i else z

    def remote(src, dst, ss, rs, dev):
        return pltpu.make_async_remote_copy(
            src_ref=src, dst_ref=dst, send_sem=ss, recv_sem=rs, device_id=dev, device_id_type=MESH
        )

    barrier = pltpu.get_barrier_semaphore()
    peers = [f(r) for f in (along_x, along_y) for r in (1, 2, 3)] + [along_z(1), along_z(-1), other_core]
    for dev in peers:
        pl.semaphore_signal(barrier, inc=1, device_id=dev, device_id_type=MESH)

    arrays = ((tok_hbm, tbuf), (go_hbm, gbuf))

    def load(a, h, i):
        cols = pl.ds(pl.multiple_of(block(h, i) * FB, FB), FB)
        return pltpu.make_async_copy(
            arrays[a][0].at[:, cols], arrays[a][1].at[h, i, pl.ds(0, TOK)], lsem.at[a, h, i]
        )

    for a in range(2):
        for i in range(4):
            for h in range(2):
                load(a, h, i).start()
    def wait_weights(m):
        src, dst = ((wg_hbm, wg), (wu_hbm, wu), (wd_hbm, wd))[m]
        for h in range(2):
            for i in range(4):
                pltpu.make_async_copy(src.at[0, :, pl.ds(0, FB)], dst.at[h, i], wsem.at[m, h, i]).wait()

    experts = lax.broadcasted_iota(jnp.int32, (NEXP, TOK), 0)
    taken = jnp.zeros((NEXP, TOK), F32)
    weight = jnp.zeros((NEXP, TOK), F32)
    for k in range(4):
        hit = routes_ref[k : k + 1, :] == experts
        taken = taken + jnp.where(hit, 1.0, 0.0)
        weight = weight + jnp.where(hit, comb_ref[k : k + 1, :], 0.0)
    earlier = (
        lax.broadcasted_iota(jnp.int32, (TOK, TOK), 0) < lax.broadcasted_iota(jnp.int32, (TOK, TOK), 1)
    ).astype(BF)
    key = jnp.where(taken > 0.5, dot(taken.astype(BF), earlier), -10000.0)
    for h in range(2):
        meta[h, 0, 0:NEXP, :] = key
        meta[h, 0, NEXP : 2 * NEXP, :] = weight

    pl.semaphore_wait(barrier, len(peers))

    for h in range(2):
        for r in (1, 2, 3):
            remote(meta.at[h, 0], meta.at[h, 4 - r], ms.at[h], mr.at[h], spread[h](r)).start()

    neighbour = (4 - 1, 1)

    def gather_own(a, h, i):
        load(a, h, i).wait()
        buf = arrays[a][1].at[h, i]
        for k, r in ((0, 1), (1, 3)) if PASS else ((0, 1), (1, 3), (2, 2)):
            remote(
                buf.at[pl.ds(0, TOK)],
                buf.at[pl.ds((4 - r) * TOK, TOK)],
                ags.at[a, h, i],
                agr.at[a, h, i, k],
                spread[h](r),
            ).start()

    def gather_pass(a, h, i):
        buf = arrays[a][1].at[h, i]
        for k, r in ((0, 1), (1, 3)):
            part = buf.at[pl.ds(neighbour[k] * TOK, TOK)]
            remote(part, part, ags.at[a, h, i], agr.at[a, h, i, k], spread[h](r)).wait_recv()
            if not PASS:
                continue
            remote(
                buf.at[pl.ds(neighbour[k] * TOK + k * (TOK // 2), TOK // 2)],
                buf.at[pl.ds(2 * TOK + k * (TOK // 2), TOK // 2)],
                ags.at[a, h, i],
                agr.at[a, h, i, 2],
                spread[h](r),
            ).start()

    def gather_far(a, h, i):
        part = arrays[a][1].at[h, i, pl.ds(2 * TOK, TOK)]
        remote(part, part, ags.at[a, h, i], agr.at[a, h, i, 2], spread[h](1)).wait_recv()

    def gather_all(a, h, i):
        part = arrays[a][1].at[h, i, pl.ds(TOK, 3 * TOK)]
        return remote(part, part, ags.at[a, h, i], agr.at[a, h, i, 0], spread[h](1))

    for n in range(LOOK):
        for h in range(2):
            gather_own(n // 4, h, n % 4)

    for m, (src, dst) in enumerate(((wg_hbm, wg), (wu_hbm, wu), (wd_hbm, wd))):
        for h in range(2):
            for i in range(4):
                cols = pl.ds(pl.multiple_of(block(h, i) * FB, FB), FB)
                pltpu.make_async_copy(src.at[0, :, cols], dst.at[h, i], wsem.at[m, h, i]).start()

    for h in range(2):
        m = meta.at[h, pl.ds(1, 3)]
        remote(m, m, ms.at[h], mr.at[h], spread[h](1)).wait()
        for r in range(4):
            ex = route[h](r)[1]
            keys = jnp.concatenate([meta[h, s, pl.ds(ex, 1), :] + float(s * CAP) for s in range(4)], axis=1)
            wts = jnp.concatenate([meta[h, s, pl.ds(ex + NEXP, 1), :] for s in range(4)], axis=1)
            hit = lax.broadcasted_iota(jnp.int32, (ROWS, 4 * TOK), 0).astype(F32) == keys
            pmat[h, r * ROWS : (r + 1) * ROWS, :] = jnp.where(hit, 1.0, 0.0).astype(BF)
            crow[h, r * ROWS : (r + 1) * ROWS, :] = jnp.sum(jnp.where(hit, wts, 0.0), axis=1, keepdims=True)

    def second_send(a, h, i):
        snd, dst = ((tsend, xin), (ssend, sin))[a]
        for r in (2, 1, 3):
            remote(
                snd.at[h, i, pl.ds(r * ROWS, ROWS)],
                dst.at[h, i, pl.ds((4 - r) * ROWS, ROWS)],
                a2s.at[a, h, i],
                a2r.at[a, h, i],
                route[h](r),
            ).start()

    def second_all(a, h, i):
        snd, dst = ((tsend, xin), (ssend, sin))[a]
        return remote(
            snd.at[h, i, pl.ds(ROWS, 3 * ROWS)],
            dst.at[h, i, pl.ds(ROWS, 3 * ROWS)],
            a2s.at[a, h, i],
            a2r.at[a, h, i],
            route[h](1),
        )

    def picked(a, h, i):
        gather_far(a, h, i)
        rows = dot(pmat[h], arrays[a][1][h, i])
        rows = (rows * crow[h] if a else rows).astype(BF)
        snd, dst = ((tsend, xin), (ssend, sin))[a]
        dst[h, i, 0:ROWS, :] = rows[0:ROWS]
        snd[h, i] = rows
        second_send(a, h, i)

    def exchange(n):
        for h in range(2):
            if n < 8 - AHEAD:
                gather_pass((n + AHEAD) // 4, h, (n + AHEAD) % 4)
            if n >= 4:
                gather_all(0, h, n - 4).wait_send()
        for h in range(2):
            picked(n // 4, h, n % 4)
        for h in range(2):
            if n >= LAG:
                second_all((n - LAG) // 4, h, (n - LAG) % 4).wait_send()
            if n < 8 - LOOK:
                gather_own((n + LOOK) // 4, h, (n + LOOK) % 4)

    def same_order(buf, i):
        val = buf[1, i].astype(F32)
        pieces = [val[p * ROWS + q * CAP : p * ROWS + (q + 1) * CAP] for q in range(4) for p in range(4)]
        buf[1, i] = jnp.concatenate(pieces, axis=0).astype(BF)

    def arrived(a, i):
        for h in range(2):
            second_all(a, h, i).wait_recv()
        same_order((xin, sin)[a], i)

    def big(r):
        return pl.ds(pl.multiple_of(r * 352, 352), 352)

    def tile(r):
        return pl.ds(pl.multiple_of(r * 176, 176), 176)

    def project(w, src, at, blocks):
        total = None
        for i in blocks:
            for h in range(2):
                term = dot(w[h, i, at, :], src[h, i], NT)
                total = term if total is None else total + term
        return total

    def gates(i):
        arrived(0, i)

        @pl.loop(0, 2)
        def _(r):
            for acc, w in ((gate, wg), (upper, wu)):
                val = project(w, xin, big(r), (i,))
                acc[big(r), :] = acc[big(r), :] + val if i else val

    def gates_end():
        @pl.loop(0, 4)
        def _(r):
            g, u = gate[tile(r), :], upper[tile(r), :]
            s = jax.nn.sigmoid(g)
            active = g * s
            hidden[tile(r), :] = (active * u).astype(BF)
            gate[tile(r), :] = u * s * (1.0 + g * (1.0 - s))
            upper[tile(r), :] = active

    outs = (out_d, out_g, out_u)

    def partial(m, h, i):
        val = dot((hidden, ggt, gut)[m][...], (sin if m == 0 else xin)[h, i])
        low, high = val[:, 0:TOK], val[:, TOK : 2 * TOK]
        own = jnp.where(c == 0, low, high)
        if h == 1 and i == 0:
            last[m] = own
        else:
            mine[m, h] = own
        csend[m, h] = jnp.where(c == 0, high, low).astype(BF)
        remote(csend.at[m, h], crecv.at[m, h, i], cs.at[m, h, i], cr.at[m, h, i], other_core).start()

    def swapped(m, h, i):
        remote(csend.at[m, h], crecv.at[m, h, i], cs.at[m, h, i], cr.at[m, h, i], other_core).wait()

    def zcopy(m, h, i, rows=pl.ds(0, HID)):
        return remote(
            zsend.at[m, h, i % 2, rows],
            zrecv.at[m, h, i, rows],
            zs.at[m, h, i],
            zr.at[m, h, i],
            along_z(1 if h == 0 else -1),
        )

    halves = (pl.ds(0, 352), pl.ds(352, 352))

    def forward(m, i):
        if i == 0:
            swapped(m, 0, 0)
            val = (mine[m, 0] + crecv[m, 0, 0].astype(F32)).astype(BF)
            for h in range(2):
                zsend[m, h, 0, halves[h], :] = val[352 * h : 352 * h + 352]
                zcopy(m, h, 0, halves[h]).start()
            return
        for h in range(2):
            swapped(m, h, i)
            if i == 1:
                zcopy(m, h, 0, halves[h]).wait_recv()
                val = mine[m, h] + crecv[m, h, 1].astype(F32)
                got = zrecv[m, h, 0, halves[h], :].astype(F32)
                keep = val[352 * (1 - h) : 352 * (1 - h) + 352]
                zsend[m, h, 1, halves[h], :] = (val[352 * h : 352 * h + 352] + got).astype(BF)
                zsend[m, h, 1, halves[1 - h], :] = keep.astype(BF)
            else:
                zcopy(m, h, i - 1).wait_recv()
                if i == 2:
                    zcopy(m, h, 0, halves[h]).wait_send()
                else:
                    zcopy(m, h, i - 2).wait_send()
                val = mine[m, h] + crecv[m, h, i].astype(F32) + zrecv[m, h, i - 1].astype(F32)
                zsend[m, h, i % 2] = val.astype(BF)
            zcopy(m, h, i).start()

    def settle(m):
        for h in range(2):
            zcopy(m, h, 3).wait_recv()
            zcopy(m, h, 2).wait_send()
            zcopy(m, h, 3).wait_send()
        near = last[m] + crecv[m, 1, 0].astype(F32)
        last[m] = near + (zrecv[m, 0, 3].astype(F32) + zrecv[m, 1, 3].astype(F32))
        pltpu.make_async_copy(last.at[m], outs[m].at[0], osem.at[m]).start()

    def back_copy(h, i, r):
        return remote(
            tsend.at[h, i, pl.ds(r * ROWS, ROWS)],
            brecv.at[h, i, pl.ds((4 - r) * ROWS, ROWS)],
            bs.at[h, i],
            br.at[h, i],
            route[h](r),
        )

    def back_all(h, i):
        return remote(
            tsend.at[h, i, pl.ds(ROWS, 3 * ROWS)],
            brecv.at[h, i, pl.ds(ROWS, 3 * ROWS)],
            bs.at[h, i],
            br.at[h, i],
            route[h](1),
        )

    def back(h, i):
        val = dot(gg[...], wg[h, i]) + dot(gu[...], wu[h, i])
        if h == 1:
            pieces = [val[p * ROWS + q * CAP : p * ROWS + (q + 1) * CAP] for q in range(4) for p in range(4)]
            val = jnp.concatenate(pieces, axis=0)
        val = val.astype(BF)
        brecv[h, i, 0:ROWS, :] = val[0:ROWS]
        tsend[h, i] = val
        for r in (2, 1, 3):
            back_copy(h, i, r).start()

    def home_all(h, i):
        return remote(
            ssend.at[h, i, pl.ds(TOK, 3 * TOK)],
            tbuf.at[h, i, pl.ds(TOK, 3 * TOK)],
            ps.at[h, i],
            pr.at[h, i],
            spread[h](1),
        )

    def home(h, i):
        back_all(h, i).wait_recv()
        if i >= 4 - LAG:
            second_all(1, h, i).wait_send()
        val = dot(pback[h], brecv[h, i]).astype(BF)
        tbuf[h, i, 0:TOK, :] = val[0:TOK]
        ssend[h, i, 0 : 4 * TOK, :] = val
        for s in (1, 3, 2):
            remote(
                ssend.at[h, i, pl.ds(s * TOK, TOK)],
                tbuf.at[h, i, pl.ds((4 - s) * TOK, TOK)],
                ps.at[h, i],
                pr.at[h, i],
                spread[h](s),
            ).start()

    def finish(h, i):
        home_all(h, i).wait_recv()
        total = tbuf[h, i, 0:TOK, :].astype(F32)
        for s in range(1, 4):
            total = total + tbuf[h, i, s * TOK : (s + 1) * TOK, :].astype(F32)
        cols = pl.ds(pl.multiple_of(block(h, i) * FB, FB), FB)
        home_rows[h, i] = total.astype(BF)
        pltpu.make_async_copy(home_rows.at[h, i], out_tok.at[:, cols], lsem.at[0, h, i]).start()

    def both(f, *args):
        f(0, *args)
        f(1, *args)

    def partials(m, i):
        partial(m, 0, i)
        partial(m, 1, i)

    def zero(m):
        partial(m, 1, 0)
        swapped(m, 1, 0)

    def down(i):
        arrived(1, i)
        partials(0, i) if i else partial(0, 0, 0)
        total = project(wd, sin, slice(None), (i,))
        gh[...] = total if i == 0 else gh[...] + total
        forward(0, i)

    for n in range(AHEAD):
        for h in range(2):
            gather_pass(0, h, n)
    exchange(0)
    exchange(1)
    exchange(2)
    wait_weights(0)
    wait_weights(1)
    gates(0)
    exchange(3)
    gates(1)
    exchange(4)
    gates(2)
    exchange(5)
    gates(3)
    gates_end()
    wait_weights(2)
    down(0)
    exchange(6)
    down(1)
    exchange(7)
    for h in range(2):
        pback[h] = pmat[h].T
    down(2)
    arrived(1, 3)
    partials(0, 3)

    @pl.loop(0, 2)
    def _(r):
        v = gh[big(r), :] + project(wd, sin, big(r), (3,))
        ggt[big(r), :] = (v * gate[big(r), :]).astype(BF)
        gut[big(r), :] = (v * upper[big(r), :]).astype(BF)

    partial(1, 0, 0)
    partial(2, 0, 0)
    forward(0, 3)
    gg[...] = ggt[...].T
    gu[...] = gut[...].T
    forward(1, 0)
    forward(2, 0)
    both(back, 0)
    partials(1, 1)
    both(back, 1)
    partials(2, 1)
    both(back, 2)
    forward(1, 1)
    forward(2, 1)
    both(back, 3)
    zero(0)
    settle(0)
    partials(1, 2)
    partials(2, 2)
    both(home, 0)
    both(home, 1)
    forward(1, 2)
    forward(2, 2)
    partials(1, 3)
    partials(2, 3)
    both(home, 2)
    both(home, 3)
    both(finish, 0)
    both(finish, 1)
    forward(1, 3)
    forward(2, 3)
    zero(1)
    zero(2)
    both(finish, 2)
    both(finish, 3)
    settle(1)
    settle(2)

    for h in range(2):
        for i in range(4):
            gather_all(1, h, i).wait_send()
            back_all(h, i).wait_send()
            home_all(h, i).wait_send()
            pltpu.make_async_copy(home_rows.at[h, i], out_tok.at[:, pl.ds(0, FB)], lsem.at[0, h, i]).wait()
    for m in range(3):
        pltpu.make_async_copy(last.at[m], outs[m].at[0], osem.at[m]).wait()


def deliver(*refs):
    for n in range(4):
        refs[4 + n][...] = refs[n][...]


def local(tokens, grad_out, routes, combine, w_gate, w_up, w_down):
    vm = pl.BlockSpec(memory_space=pltpu.VMEM)
    hbm = pl.BlockSpec(memory_space=pl.ANY)
    grad = jax.ShapeDtypeStruct((1, HID, TOK), F32)
    shapes = (jax.ShapeDtypeStruct((TOK, WID), BF), grad, grad, grad)
    sem = pltpu.SemaphoreType.DMA
    V = pltpu.VMEM
    parts = pl.pallas_call(
        kernel,
        name="experts",
        out_shape=shapes,
        in_specs=[hbm, hbm, vm, vm, hbm, hbm, hbm],
        out_specs=(hbm, hbm, hbm, hbm),
        scratch_shapes=[
            V((2, 4, HID, FB), BF), V((2, 4, HID, FB), BF), V((2, 4, HID, FB), BF),
            V((2, 4, 2 * NEXP, 128), F32),
            V((2, ALL, 4 * TOK), BF), V((2, 4 * TOK, ALL), BF),
            V((2, ALL, 1), F32),
            V((2, 4, 4 * TOK, FB), BF), V((2, 4, 4 * TOK, FB), BF),
            V((2, 4, ALL, FB), BF), V((2, 4, ALL, FB), BF),
            V((2, 4, ALL, FB), BF), V((2, 4, ALL, FB), BF),
            V((HID, ALL), F32), V((HID, ALL), F32), V((HID, ALL), F32),
            V((HID, ALL), BF), V((HID, ALL), BF), V((HID, ALL), BF),
            V((ALL, HID), BF), V((ALL, HID), BF),
            V((3, 2, HID, TOK), F32), V((3, HID, TOK), F32),
            V((3, 2, HID, TOK), BF),
            V((3, 2, 4, HID, TOK), BF),
            V((3, 2, 2, HID, TOK), BF),
            V((3, 2, 4, HID, TOK), BF),
            V((2, 4, ALL, FB), BF),
            V((2, 4, TOK, FB), BF),
            sem((3, 2, 4)), sem((2, 2, 4)), sem((3,)), sem((2,)), sem((2,)),
            sem((2, 2, 4)), sem((2, 2, 4, 3)), sem((2, 2, 4)), sem((2, 2, 4)),
            sem((3, 2, 4)), sem((3, 2, 4)), sem((3, 2, 4)), sem((3, 2, 4)),
            sem((2, 4)), sem((2, 4)), sem((2, 4)), sem((2, 4)),
        ],
        compiler_params=pltpu.CompilerParams(
            collective_id=0, has_side_effects=True, vmem_limit_bytes=62 * 2**20
        ),
        cost_estimate=pl.CostEstimate(flops=15 * 10**9, bytes_accessed=12 * 10**6, transcendentals=450560),
    )(tokens, grad_out, routes.T, combine.T, *[w.transpose(0, 2, 1) for w in (w_gate, w_up, w_down)])
    grad_tokens, *grads = pl.pallas_call(
        deliver,
        name="deliver",
        out_shape=shapes,
        in_specs=[vm] * 4,
        out_specs=(vm,) * 4,
    )(*parts)
    return (grad_tokens, *[g.transpose(0, 2, 1) for g in grads])


def solution(mesh):
    rows = P(("dp", "expert"), None)
    weights = P("expert", None, None)
    grads = P("expert", "dp", None)
    return jax.shard_map(
        local,
        mesh=mesh,
        in_specs=(rows, rows, rows, rows, weights, weights, weights),
        out_specs=(rows, grads, grads, grads),
        check_vma=False,
    )
```

time: 151 us -> 112 us (0.74)
  local copies, waits for them, and re-layouts: 22.6 us -> 0 us
  Pallas kernels: 128 us -> 111 us
    unnamed x8 -> x0, local copies, waits for them, and re-layouts: 16.9 us -> none
    pallas_call x1 -> x2, Pallas kernels: 128 us -> 111 us  [the longest x1 109 us: local(): pl.pallas_call(kernel, name='experts', out_shape=shapes, in_specs=[hbm, h...]
    pallas_call x3 -> x0, local copies, waits for them, and re-layouts: 5.69 us -> none  [local(): pl.pallas_call(kernel, name='experts', out_shape=(jax.ShapeDtypeStruct((T...]
where the time goes in v2:
time: 112 us
  Pallas kernels  111 us (99%)
    pallas_call x1, Pallas kernels, local(): pl.pallas_call(kernel, name='experts', out_shape=shapes, in_specs=[hbm, h...  109 us
    pallas_call x1, Pallas kernels, local(): pl.pallas_call(deliver, name='deliver', out_shape=shapes, in_specs=[vm] *...  2.53 us

profile of v2, /device:TPU:1, one launch (start us, length us, event | category | flops | bytes accessed | tf_op | source)
XLA Modules:
  0.0 111.9 jit_solution(11556512023104414406)
XLA Ops:
  0.6 108.7 %experts.1 = (bf16[128,2048]{1,0:T(8,128)(2,1)}, f32[1,704,128]{2,1,0:T(8,128)}, f32[1,704,128]{2,1,0:T(8,128)}, f32[1,704,128]{2,1,0:T(8,128)}) custom-call(bf16[128,2048]{1,0:T(8,128)(2,1)} %tok_hbm.1, bf16[128,2048]{1,0:T(8,128)(2,1)} %go_hbm.1, s32[4,128]{1,0:T(4,128)} %bitcast.14, f32[4,128]{1,0:T(4,128)} %bitcast.15, bf16[1,704,2048]{2,1,0:T(8,128)(2,1)} %bitcast.8, ...), custom_call_target="tpu_custom_call" | custom-call | flops 15000000512 | bytes 12000000 | tf_op jit(solution)/shard_map/experts/pallas_call | solution.py:487
  109.3 2.5 %deliver.1 = (bf16[128,2048]{1,0:T(8,128)(2,1)}, f32[1,704,128]{2,1,0:T(8,128)}, f32[1,704,128]{2,1,0:T(8,128)}, f32[1,704,128]{2,1,0:T(8,128)}) custom-call(bf16[128,2048]{1,0:T(8,128)(2,1)} %get-tuple-element.12.refs_0_, f32[1,704,128]{2,1,0:T(8,128)} %get-tuple-element.13.refs_1_, f32[1,704,128]{2,1,0:T(8,128)} %get-tuple-element.14.refs_2_, ...), custom_call_target="tpu_custom_call" | custom-call | tf_op jit(solution)/shard_map/deliver/pallas_call | solution.py:521

commit v3 on v2

--- a/solution.py
+++ b/solution.py
@@ -426,40 +426,40 @@
 
     partial(1, 0, 0)
     partial(2, 0, 0)
-    forward(0, 3)
     gg[...] = ggt[...].T
     gu[...] = gut[...].T
     forward(1, 0)
+    forward(0, 3)
     forward(2, 0)
     both(back, 0)
     partials(1, 1)
     both(back, 1)
+    forward(1, 1)
     partials(2, 1)
     both(back, 2)
-    forward(1, 1)
     forward(2, 1)
+    partials(1, 2)
     both(back, 3)
     zero(0)
+    forward(1, 2)
+    partials(2, 2)
     settle(0)
-    partials(1, 2)
-    partials(2, 2)
     both(home, 0)
-    both(home, 1)
-    forward(1, 2)
     forward(2, 2)
     partials(1, 3)
+    both(home, 1)
+    forward(1, 3)
     partials(2, 3)
     both(home, 2)
+    forward(2, 3)
     both(home, 3)
+    zero(1)
     both(finish, 0)
     both(finish, 1)
-    forward(1, 3)
-    forward(2, 3)
-    zero(1)
+    settle(1)
     zero(2)
     both(finish, 2)
     both(finish, 3)
-    settle(1)
     settle(2)
 
     for h in range(2):
@@ -473,8 +473,16 @@
 
 
 def deliver(*refs):
+    ins, outs, held, sems = refs[0:4], refs[4:8], refs[8:12], refs[12]
+    copies = [pltpu.make_async_copy(ins[n], held[n], sems.at[0, n]) for n in range(4)]
+    back = [pltpu.make_async_copy(held[n], outs[n], sems.at[1, n]) for n in range(4)]
+    for copy in copies:
+        copy.start()
     for n in range(4):
-        refs[4 + n][...] = refs[n][...]
+        copies[n].wait()
+        back[n].start()
+    for copy in back:
+        copy.wait()
 
 
 def local(tokens, grad_out, routes, combine, w_gate, w_up, w_down):
@@ -522,8 +530,9 @@
         deliver,
         name="deliver",
         out_shape=shapes,
-        in_specs=[vm] * 4,
-        out_specs=(vm,) * 4,
+        in_specs=[hbm] * 4,
+        out_specs=(hbm,) * 4,
+        scratch_shapes=[V(o.shape, o.dtype) for o in shapes] + [sem((2, 4))],
     )(*parts)
     return (grad_tokens, *[g.transpose(0, 2, 1) for g in grads])
 

time: 112 us -> 108 us (0.964)
  Pallas kernels: 111 us -> 107 us
    pallas_call x1, Pallas kernels: 109 us -> 105 us  [local(): pl.pallas_call(kernel, name='experts', out_shape=shapes, in_specs=[hbm, h...]
where the time goes in v3:
time: 108 us
  Pallas kernels  107 us (99%)
    pallas_call x1, Pallas kernels, local(): pl.pallas_call(kernel, name='experts', out_shape=shapes, in_specs=[hbm, h...  105 us
    pallas_call x1, Pallas kernels, local(): pl.pallas_call(deliver, name='deliver', out_shape=shapes, in_specs=[hbm]...  2.26 us

profile of v3, /device:TPU:1, one launch (start us, length us, event | category | flops | bytes accessed | tf_op | source)
XLA Modules:
  0.0 107.8 jit_solution(12534365741928091060)
XLA Ops:
  0.6 104.7 %experts.1 = (bf16[128,2048]{1,0:T(8,128)(2,1)}, f32[1,704,128]{2,1,0:T(8,128)}, f32[1,704,128]{2,1,0:T(8,128)}, f32[1,704,128]{2,1,0:T(8,128)}) custom-call(bf16[128,2048]{1,0:T(8,128)(2,1)} %tok_hbm.1, bf16[128,2048]{1,0:T(8,128)(2,1)} %go_hbm.1, s32[4,128]{1,0:T(4,128)} %bitcast.14, f32[4,128]{1,0:T(4,128)} %bitcast.15, bf16[1,704,2048]{2,1,0:T(8,128)(2,1)} %bitcast.8, ...), custom_call_target="tpu_custom_call" | custom-call | flops 15000000512 | bytes 12000000 | tf_op jit(solution)/shard_map/experts/pallas_call | solution.py:495
  105.4 2.3 %deliver.1 = (bf16[128,2048]{1,0:T(8,128)(2,1)}, f32[1,704,128]{2,1,0:T(8,128)}, f32[1,704,128]{2,1,0:T(8,128)}, f32[1,704,128]{2,1,0:T(8,128)}) custom-call(bf16[128,2048]{1,0:T(8,128)(2,1)} %get-tuple-element.12.refs_0_, f32[1,704,128]{2,1,0:T(8,128)} %get-tuple-element.13.refs_1_, f32[1,704,128]{2,1,0:T(8,128)} %get-tuple-element.14.refs_2_, ...), custom_call_target="tpu_custom_call" | custom-call | tf_op jit(solution)/shard_map/deliver/pallas_call | solution.py:529

commit v4 on v3

--- a/solution.py
+++ b/solution.py
@@ -416,7 +416,6 @@
         pback[h] = pmat[h].T
     down(2)
     arrived(1, 3)
-    partials(0, 3)
 
     @pl.loop(0, 2)
     def _(r):
@@ -426,6 +425,7 @@
 
     partial(1, 0, 0)
     partial(2, 0, 0)
+    partials(0, 3)
     gg[...] = ggt[...].T
     gu[...] = gut[...].T
     forward(1, 0)

time: 108 us -> 108 us (level)
  no operation moved by 1% of the time
where the time goes in v4:
time: 108 us
  Pallas kernels  107 us (99%)
    pallas_call x1, Pallas kernels, local(): pl.pallas_call(kernel, name='experts', out_shape=shapes, in_specs=[hbm, h...  105 us
    pallas_call x1, Pallas kernels, local(): pl.pallas_call(deliver, name='deliver', out_shape=shapes, in_specs=[hbm]...  2.26 us

profile of v4, /device:TPU:1, one launch (start us, length us, event | category | flops | bytes accessed | tf_op | source)
XLA Modules:
  0.0 107.6 jit_solution(4524955535346902925)
XLA Ops:
  0.6 104.5 %experts.1 = (bf16[128,2048]{1,0:T(8,128)(2,1)}, f32[1,704,128]{2,1,0:T(8,128)}, f32[1,704,128]{2,1,0:T(8,128)}, f32[1,704,128]{2,1,0:T(8,128)}) custom-call(bf16[128,2048]{1,0:T(8,128)(2,1)} %tok_hbm.1, bf16[128,2048]{1,0:T(8,128)(2,1)} %go_hbm.1, s32[4,128]{1,0:T(4,128)} %bitcast.14, f32[4,128]{1,0:T(4,128)} %bitcast.15, bf16[1,704,2048]{2,1,0:T(8,128)(2,1)} %bitcast.8, ...), custom_call_target="tpu_custom_call" | custom-call | flops 15000000512 | bytes 12000000 | tf_op jit(solution)/shard_map/experts/pallas_call | solution.py:495
  105.2 2.3 %deliver.1 = (bf16[128,2048]{1,0:T(8,128)(2,1)}, f32[1,704,128]{2,1,0:T(8,128)}, f32[1,704,128]{2,1,0:T(8,128)}, f32[1,704,128]{2,1,0:T(8,128)}) custom-call(bf16[128,2048]{1,0:T(8,128)(2,1)} %get-tuple-element.12.refs_0_, f32[1,704,128]{2,1,0:T(8,128)} %get-tuple-element.13.refs_1_, f32[1,704,128]{2,1,0:T(8,128)} %get-tuple-element.14.refs_2_, ...), custom_call_target="tpu_custom_call" | custom-call | tf_op jit(solution)/shard_map/deliver/pallas_call | solution.py:529
